TPU v7x, 128 devices: a whole 4x4x4 slice. The times are simulated.
128 devices in a mesh: wide: 16 (over z, x), narrow: 8 (over y, core).
Axes of the slice: x: 4, y: 4, z: 4, core: 2. Of those that a mesh axis runs over, the one named last changes fastest.
Arguments:
- cotangent: float32 [1536, 256, 256], P(('wide', 'narrow')), may hold values from -6 to 6
- row_basis: float32 [1536, 256, 128], P(('wide', 'narrow')), may hold values from -0.375 to 0.375
- col_basis: float32 [1536, 256, 128], P(('wide', 'narrow')), may hold values from -0.5 to 0.5
- leaf_up: float32 [1536, 128, 128], P(('wide', 'narrow')), may hold values from -0.15625 to 0.15625
- node_up: float32 [128, 128, 128], P(('wide', 'narrow')), may hold values from -0.1875 to 0.1875
- node_couple: float32 [128, 2, 128, 128], P(('wide', 'narrow')), may hold values from -0.375 to 0.375
- group_couple: float32 [16, 8, 128, 128], P('wide', 'narrow'), may hold values from -0.1875 to 0.1875
- node_down: float32 [128, 128, 128], P(('wide', 'narrow')), may hold values from -0.5 to 0.5
- leaf_down: float32 [1536, 128, 128], P(('wide', 'narrow')), may hold values from -0.5 to 0.5
- near_blocks: float32 [1536, 4, 256, 256], P(('wide', 'narrow')), may hold values from -0.1875 to 0.1875
- near_index: int32 [1536, 4], P(('wide', 'narrow')), may hold values from 0 to 1535, as said below
- far_nodes: int32 [128, 2], P(('wide', 'narrow')), may hold values from 0 to 7, as said below
- far_groups: int32 [16, 8], P('wide', 'narrow'), may hold values from 0 to 15, as said below
Outputs:
- product: float32 [1536, 256, 256], P(('wide', 'narrow'))
Inputs may be any that keep to these rules, and one draw needn't show every extreme that they name: near_index[l, 0] is l; every other entry differs from l by 1 to 2. far_nodes[d, j] never equals d % 8; the entries of a row differ. far_groups[g, j] never equals g; the entries of a row differ.
All inputs are finite; a program needn't handle non-finite values.
Results may differ from a plain program's by a relative error of at most 0.000062.
Values sent between devices are 32-bit elements; how exact they have to be, the bound alone decides.
A program may use at most 128 MiB of HBM per device.

v0:
```python
import jax
import jax.numpy as jnp
from jax import lax
from jax.sharding import PartitionSpec as P

NEAR_REACH = 2
HIGH = lax.Precision.HIGHEST


def from_behind(value, axis, steps):
    count = lax.axis_size(axis)
    leading, last = (max(0, -steps), min(count, count - steps))
    return lax.ppermute(value, axis, [(source, source + steps) for source in range(leading, last)])


def shards(
    cotangent,
    row_basis,
    col_basis,
    leaf_up,
    node_up,
    node_couple,
    group_couple,
    node_down,
    leaf_down,
    near_blocks,
    near_index,
    far_nodes,
    far_groups,
):
    leaves = cotangent.shape[0]
    lower = from_behind(cotangent[leaves - NEAR_REACH :], ("wide", "narrow"), 1)
    upper = from_behind(cotangent[:NEAR_REACH], ("wide", "narrow"), -1)
    leaf_coeffs = jnp.einsum("lpk,lpv->lkv", row_basis, cotangent, precision=HIGH)
    node_coeffs = jnp.einsum("lkm,lkv->mv", leaf_up, leaf_coeffs, precision=HIGH)
    up_term = jnp.dot(node_up[0].T, node_coeffs, precision=HIGH)
    siblings = lax.all_gather(node_coeffs[None], "narrow", axis=0, tiled=True)
    group_coeffs = lax.psum(up_term, "narrow")
    picked = siblings[far_nodes[0]]
    node_out = jnp.einsum("jkm,jkv->mv", node_couple[0], picked, precision=HIGH)
    all_groups = lax.all_gather(group_coeffs[None], "wide", axis=0, tiled=True)
    picked_groups = all_groups[far_groups[0]]
    partial_value = jnp.einsum("jkm,jkv->mv", group_couple[0], picked_groups, precision=HIGH)
    group_out = lax.psum(partial_value, "narrow")
    node_total = node_out + jnp.dot(node_down[0], group_out, precision=HIGH)
    leaf_total = jnp.einsum("lmk,kv->lmv", leaf_down, node_total, precision=HIGH)
    far_part = jnp.einsum("lpk,lkv->lpv", col_basis, leaf_total, precision=HIGH)
    extended = jnp.concatenate([lower, cotangent, upper], axis=0)
    node_rank = lax.axis_index("wide") * lax.axis_size("narrow") + lax.axis_index("narrow")
    first_leaf = node_rank * leaves - NEAR_REACH
    local_index = near_index - first_leaf
    sources = extended[local_index]
    near_part = jnp.einsum("ljpq,ljpv->lqv", near_blocks, sources, precision=HIGH)
    return far_part + near_part


def solution(mesh):
    in_specs = (
        P(("wide", "narrow"), None, None),
        P(("wide", "narrow"), None, None),
        P(("wide", "narrow"), None, None),
        P(("wide", "narrow"), None, None),
        P(("wide", "narrow"), None, None),
        P(("wide", "narrow"), None, None, None),
        P("wide", "narrow", None, None),
        P(("wide", "narrow"), None, None),
        P(("wide", "narrow"), None, None),
        P(("wide", "narrow"), None, None, None),
        P(("wide", "narrow"), None),
        P(("wide", "narrow"), None),
        P("wide", "narrow"),
    )
    out_specs = P(("wide", "narrow"), None, None)
    return jax.shard_map(shards, mesh=mesh, in_specs=in_specs, out_specs=out_specs, check_vma=False)
```

profile of v0, /device:TPU:0, one launch (start us, length us, event | category | flops | bytes accessed | tf_op | source)
XLA Modules:
  0.0 259.9 jit_solution(13110974289088481287)
XLA Ops:
  6.5 7.7 %fusion.14 = f32[12,128,256]{1,2,0:T(8,128)S(1)} fusion(f32[12,256,128]{2,1,0:T(8,128)} %param.14, f32[12,256,256]{2,1,0:T(8,128)} %param.13), kind=kOutput, calls=%fused_computation.26 | convolution fusion | flops 1207959552 | bytes 6291456 | tf_op jit(solution)/shard_map/lpk,lpv->lkv/dot_general | solution.py:34
  14.3 1.4 fusion.15
  15.7 0.9 convolution_bitcast_fusion.2
  16.6 0.0 all-reduce.3.cloned.1.call-update
  16.7 0.0 all-gather.6.cloned.1.call-start
  16.7 0.7 all-gather.6.cloned.1.call-update
  17.4 0.0 all-gather.4.cloned.1.call-start
  17.5 61.0 %all-reduce.3.cloned.1.call-done = f32[1,128,256]{1,2,0:T(8,128)} async-done(((f32[1,128,256]{1,2,0:T(8,128)}), f32[1,128,256]{1,2,0:T(8,128)}) %all-reduce.3.cloned.1.call-update) | async-done | bytes 131088 | tf_op jit(solution)/shard_map/psum | solution.py:38
  78.5 1.7 copy.25
  80.2 0.0 all-gather.4.cloned.1.call-update
  80.2 0.0 all-reduce.5.cloned.1.call-start
  80.2 2.1 fusion.13
  82.3 1.3 collective-permute-start
  83.7 1.5 collective-permute-start.1
  85.8 0.1 copy.26
  85.9 0.1 reshape.69
  86.1 1.4 collective-permute-done.1
  87.5 4.3 %pad_maximum_fusion = f32[16,256,256]{2,1,0:T(8,128)} fusion(f32[2,256,256]{2,1,0:T(8,128)S(1)} %collective-permute-done.1, f32[12,256,256]{2,1,0:T(8,128)} %param.13, f32[2,256,256]{2,1,0:T(8,128)S(1)} %collective-permute-done), kind=kLoop, calls=%fused_computation.2 | loop fusion | flops 2097152 | bytes 8388608 | tf_op jit(solution)/shard_map/concatenate | solution.py:48
  91.7 10.0 %gather_fusion.1 = f32[48,256,256]{2,1,0:T(8,128)} fusion(f32[16,256,256]{2,1,0:T(8,128)} %pad_maximum_fusion, s32[1024]{0:T(1024)S(1)} %pad_clamp_fusion), kind=kCustom, calls=%fused_computation.1 | custom fusion | bytes 25166016 | tf_op jit(solution)/shard_map/gather | solution.py:52
  101.8 5.8 %all-gather.6.cloned.1.call-done = f32[1024,256]{0,1:T(8,128)} async-done(((f32[128,256]{0,1:T(8,128)}), f32[1024,256]{0,1:T(8,128)}) %all-gather.6.cloned.1.call-update) | async-done | bytes 1048592 | tf_op jit(solution)/shard_map/all_gather | solution.py:37
  107.6 1.6 copy.34
  109.2 0.6 gather_fusion
  109.7 45.5 %all-gather.4.cloned.1.call-done = f32[16,128,256]{2,1,0:T(8,128)} async-done(((f32[1,128,256]{2,1,0:T(8,128)}), f32[16,128,256]{2,1,0:T(8,128)}) %all-gather.4.cloned.1.call-update) | async-done | bytes 2097168 | tf_op jit(solution)/shard_map/all_gather | solution.py:41
  155.2 1.9 convolution_bitcast_fusion.1
  157.2 0.0 all-reduce.5.cloned.1.call-update
  157.2 0.6 convolution_bitcast_fusion
  157.8 58.3 %all-reduce.5.cloned.1.call-done = f32[128,256]{0,1:T(8,128)} async-done(((f32[128,256]{0,1:T(8,128)}), f32[128,256]{0,1:T(8,128)}) %all-reduce.5.cloned.1.call-update) | async-done | bytes 131088 | tf_op jit(solution)/shard_map/psum | solution.py:44
  216.1 1.2 fusion.3
  217.3 2.5 fusion.16
  219.9 2.9 %fusion.1 = f32[12,256,256]{2,1,0:T(8,128)S(1)} fusion(f32[12,256,128]{2,1,0:T(8,128)S(1)} %copy-done, f32[256,12,128]{2,0,1:T(8,128)S(1)} %fusion.16), kind=kOutput, calls=%fused_computation.5 | convolution fusion | flops 1207959552 | bytes 6291456 | tf_op jit(solution)/shard_map/lpk,lkv->lpv/dot_general | solution.py:47
  222.8 27.0 %fusion = f32[12,256,256]{1,2,0:T(8,128)} fusion(f32[12,256,256]{2,1,0:T(8,128)S(1)} %fusion.1, f32[12,4,256,256]{3,2,1,0:T(8,128)} %bitcast.62, f32[12,4,256,256]{3,2,1,0:T(8,128)} %param.22), kind=kOutput, calls=%fused_computation.4 | convolution fusion | flops 9664462848 | bytes 31457280 | tf_op jit(solution)/shard_map/ljpq,ljpv->lqv/dot_general | solution.py:53
  249.8 3.5 %copy.28 = f32[12,256,256]{2,1,0:T(8,128)} copy(f32[12,256,256]{1,2,0:T(8,128)} %fusion) | data formatting | bytes 6291456 | tf_op jit(solution)/shard_map/add | solution.py:54
  (24 shorter events, 0.1 us)
Async XLA Ops:
  6.5 213.3 %copy-start = (f32[12,256,128]{2,1,0:T(8,128)S(1)}, f32[12,256,128]{2,1,0:T(8,128)}, u32[]{:S(2)}) copy-start(f32[12,256,128]{2,1,0:T(8,128)} %param.15) | copy-start | bytes 4718596
  6.5 7.7 %copy-start.2 = (f32[12,128,128]{2,1,0:T(8,128)S(1)}, f32[12,128,128]{2,1,0:T(8,128)}, u32[]{:S(2)}) copy-start(f32[12,128,128]{2,1,0:T(8,128)} %param.16) | copy-start | bytes 2359300
  6.5 9.2 %copy-start.4 = (f32[1,128,128]{2,1,0:T(8,128)S(1)}, f32[1,128,128]{2,1,0:T(8,128)}, u32[]{:S(2)}) copy-start(f32[1,128,128]{2,1,0:T(8,128)} %param.17) | copy-start | bytes 196612
  6.5 72.0 %all-reduce.3.cloned.1.call-start = ((), (), s32[]{:S(2)}) async-start(), calls=%async_computation | async-start | bytes 262144 | tf_op jit(solution)/shard_map/psum | solution.py:38
  14.3 70.9 %copy-start.7 = (s32[12,4]{0,1:T(4,128)S(1)}, s32[12,4]{0,1:T(4,128)}, u32[]{:S(2)}) copy-start(s32[12,4]{0,1:T(4,128)} %param.23) | copy-start | bytes 580
  14.3 71.7 %copy-start.8 = (s32[1,2]{1,0:T(1,128)S(1)}, s32[1,2]{1,0:T(1,128)}, u32[]{:S(2)}) copy-start(s32[1,2]{1,0:T(1,128)} %param.24) | copy-start | bytes 28
  15.7 1.0 copy-start.1
  16.7 90.9 %all-gather.6.cloned.1.call-start = ((), (), s32[]{:S(2)}) async-start(), calls=%async_computation.3 | async-start | bytes 1179648 | tf_op jit(solution)/shard_map/all_gather | solution.py:37
  17.4 137.8 %all-gather.4.cloned.1.call-start = ((), (), s32[]{:S(2)}) async-start(), calls=%async_computation.1 | async-start | bytes 2228224 | tf_op jit(solution)/shard_map/all_gather | solution.py:41
  80.2 135.9 %all-reduce.5.cloned.1.call-start = ((), (), s32[]{:S(2)}) async-start(), calls=%async_computation.2 | async-start | bytes 262144 | tf_op jit(solution)/shard_map/psum | solution.py:44
  82.3 3.7 %collective-permute-start = (f32[2,256,256]{2,1,0:T(8,128)}, f32[2,256,256]{2,1,0:T(8,128)S(1)}, u32[]{:S(2)}, u32[]{:S(2)}) collective-permute-start(f32[2,256,256]{2,1,0:T(8,128)} %get-tuple-element.16), channel_id=1, source_target_pairs={{0,1},{1,2},{2,3},{3,4},{4,5},{5,6},{6,7},{7,8},{8,9},{9,10},{10,1... | collective-permute-start | bytes 1572872 | tf_op jit(solution)/shard_map/ppermute | solution.py:13
  83.7 3.8 %collective-permute-start.1 = (f32[2,256,256]{2,1,0:T(8,128)S(1)}, f32[2,256,256]{2,1,0:T(8,128)S(1)}, u32[]{:S(2)}, u32[]{:S(2)}) collective-permute-start(f32[2,256,256]{2,1,0:T(8,128)S(1)} %get-tuple-element.17), channel_id=1, source_target_pairs={{1,0},{2,1},{3,2},{4,3},{5,4},{6,5},{7,6},{8,7},{9,8},{10,9},{11,1... | collective-permute-start | bytes 1572872 | tf_op jit(solution)/shard_map/ppermute | solution.py:13
  91.7 63.5 %copy-start.5 = (f32[1,1,128,128]{3,2,1,0:T(8,128)S(1)}, f32[1,1,128,128]{3,2,1,0:T(8,128)}, u32[]{:S(2)}) copy-start(f32[1,1,128,128]{3,2,1,0:T(8,128)} %param.19) | copy-start | bytes 196612
  101.8 55.5 %copy-start.3 = (f32[1,2,128,128]{3,2,1,0:T(8,128)S(1)}, f32[1,2,128,128]{3,2,1,0:T(8,128)}, u32[]{:S(2)}) copy-start(f32[1,2,128,128]{3,2,1,0:T(8,128)} %param.18) | copy-start | bytes 393220
  101.8 114.4 %copy-start.6 = (f32[1,128,128]{2,1,0:T(8,128)S(1)}, f32[1,128,128]{2,1,0:T(8,128)}, u32[]{:S(2)}) copy-start(f32[1,128,128]{2,1,0:T(8,128)} %param.20) | copy-start | bytes 196612
Sparse Core Ops, SparseCore 0:
  16.8 61.6 all-reduce.2
  80.3 27.2 all-gather.5
  110.0 45.2 all-gather.3
  157.5 58.5 all-reduce.4
where the time goes:
time: 260 us
  waiting for transfers between devices  173 us (67%)
  matrix products  46.2 us (18%)
  local copies, waits for them, and re-layouts  19.7 us (8%)
  between operations  14 us (5%)
  other arithmetic  4.28 us (2%)
  starting transfers between devices  2.91 us (1%)
    psum x1, waiting for transfers between devices, shards(): group_coeffs = lax.psum(up_term, 'narrow')  61 us
    psum x1, waiting for transfers between devices, shards(): group_out = lax.psum(partial_value, 'narrow')  58.3 us
    all_gather x1, waiting for transfers between devices, shards(): all_groups = lax.all_gather(group_coeffs[None], 'wide', axis=0, tiled=True)  45.5 us
    dot_general x1, matrix products, shards(): jnp.einsum('ljpq,ljpv->lqv', near_blocks, sources, precision=HIGH)  27 us
    gather x1, local copies, waits for them, and re-layouts, shards(): sources = extended[local_index]  10 us
    dot_general x1, matrix products, shards(): jnp.einsum('lpk,lpv->lkv', row_basis, cotangent, precision=HIGH)  7.71 us
    all_gather x1, waiting for transfers between devices, shards(): siblings = lax.all_gather(node_coeffs[None], 'narrow', axis=0, tiled=True)  5.84 us
  transfers between devices with their start and end apart: 6, of which 5 were waited for; matrix products, arithmetic and copies ran while one was open for 8% of the time, Pallas kernels for 0%

commit v1 on v0

--- a/solution.py
+++ b/solution.py
@@ -41,7 +41,7 @@
     all_groups = lax.all_gather(group_coeffs[None], "wide", axis=0, tiled=True)
     picked_groups = all_groups[far_groups[0]]
     partial_value = jnp.einsum("jkm,jkv->mv", group_couple[0], picked_groups, precision=HIGH)
-    group_out = lax.psum(partial_value, "narrow")
+    group_out = jnp.sum(lax.all_gather(partial_value, "narrow"), axis=0)
     node_total = node_out + jnp.dot(node_down[0], group_out, precision=HIGH)
     leaf_total = jnp.einsum("lmk,kv->lmv", leaf_down, node_total, precision=HIGH)
     far_part = jnp.einsum("lpk,lkv->lpv", col_basis, leaf_total, precision=HIGH)

time: 260 us -> 224 us (0.86)
  waiting for transfers between devices: 173 us -> 136 us
    psum x1 -> x0, waiting for transfers between devices: 58.3 us -> none  [shards(): group_out = lax.psum(partial_value, 'narrow')]
    all_gather x0 -> x1, waiting for transfers between devices: none -> 21.9 us  [shards(): group_out = jnp.sum(lax.all_gather(partial_value, 'narrow'), axis=0)]
  transfers between devices with their start and end apart: 6 -> 6, of which waited for: 5 -> 5; matrix products, arithmetic and copies ran while one was open for 8% -> 9% of each run, Pallas kernels for 0% -> 0%
where the time goes in v1:
time: 224 us; the launch traced here: 222 us
  waiting for transfers between devices  136 us (61%)
  matrix products  44.1 us (20%)
  local copies, waits for them, and re-layouts  21 us (9%)
  between operations  14 us (6%)
  other arithmetic  4.48 us (2%)
  starting transfers between devices  2.91 us (1%)
    psum x1, waiting for transfers between devices, shards(): group_coeffs = lax.psum(up_term, 'narrow')  61.9 us
    all_gather x1, waiting for transfers between devices, shards(): all_groups = lax.all_gather(group_coeffs[None], 'wide', axis=0, tiled=True)  43.6 us
    dot_general x1, matrix products, shards(): jnp.einsum('ljpq,ljpv->lqv', near_blocks, sources, precision=HIGH)  27 us
    all_gather x1, waiting for transfers between devices, shards(): group_out = jnp.sum(lax.all_gather(partial_value, 'narrow'), axis=0)  21.9 us
    gather x1, local copies, waits for them, and re-layouts, shards(): sources = extended[local_index]  9.98 us
    dot_general x1, matrix products, shards(): jnp.einsum('lpk,lpv->lkv', row_basis, cotangent, precision=HIGH)  7.71 us
  transfers between devices with their start and end apart: 6, of which 5 were waited for; matrix products, arithmetic and copies ran while one was open for 9% of the time, Pallas kernels for 0%

profile of v1, /device:TPU:0, one launch (start us, length us, event | category | flops | bytes accessed | tf_op | source)
XLA Modules:
  0.0 222.3 jit_solution(2226433421824706752)
XLA Ops:
  6.5 7.7 %fusion.14 = f32[12,128,256]{1,2,0:T(8,128)S(1)} fusion(f32[12,256,128]{2,1,0:T(8,128)} %param.14, f32[12,256,256]{2,1,0:T(8,128)} %param.13), kind=kOutput, calls=%fused_computation.27 | convolution fusion | flops 1207959552 | bytes 6291456 | tf_op jit(solution)/shard_map/lpk,lpv->lkv/dot_general | solution.py:34
  14.3 1.4 fusion.15
  15.7 0.9 convolution_bitcast_fusion.2
  16.7 0.0 all-reduce.2.cloned.1.call-update
  16.7 0.0 all-gather.6.cloned.1.call-start
  16.7 61.9 %all-reduce.2.cloned.1.call-done = f32[1,128,256]{1,2,0:T(8,128)} async-done(((f32[1,128,256]{1,2,0:T(8,128)}), f32[1,128,256]{1,2,0:T(8,128)}) %all-reduce.2.cloned.1.call-update) | async-done | bytes 131088 | tf_op jit(solution)/shard_map/psum | solution.py:38
  78.6 1.7 copy.25
  80.3 0.0 all-gather.8.cloned.1.call-start
  80.4 0.7 all-gather.8.cloned.1.call-update
  81.0 0.0 all-gather.10.cloned.1.call-start
  81.7 43.6 %all-gather.6.cloned.1.call-done = f32[16,128,256]{2,1,0:T(8,128)} async-done(((f32[1,128,256]{2,1,0:T(8,128)}), f32[16,128,256]{2,1,0:T(8,128)}) %all-gather.6.cloned.1.call-update) | async-done | bytes 2097168 | tf_op jit(solution)/shard_map/all_gather | solution.py:41
  125.3 1.9 convolution_bitcast_fusion.1
  127.3 2.1 fusion.13
  129.3 1.3 collective-permute-start
  130.7 1.5 collective-permute-start.1
  132.2 0.1 copy.26
  132.3 0.1 reshape.69
  132.4 3.7 %collective-permute-done.1 = f32[2,256,256]{2,1,0:T(8,128)S(1)} collective-permute-done((f32[2,256,256]{2,1,0:T(8,128)S(1)}, f32[2,256,256]{2,1,0:T(8,128)S(1)}, u32[]{:S(2)}, u32[]{:S(2)}) %collective-permute-start.1) | collective-permute-done | bytes 524320 | tf_op jit(solution)/shard_map/ppermute | solution.py:13
  136.2 4.2 %pad_maximum_fusion = f32[16,256,256]{2,1,0:T(8,128)} fusion(f32[2,256,256]{2,1,0:T(8,128)S(1)} %collective-permute-done.1, f32[12,256,256]{2,1,0:T(8,128)} %param.13, f32[2,256,256]{2,1,0:T(8,128)S(1)} %collective-permute-done), kind=kLoop, calls=%fused_computation.2 | loop fusion | flops 2097152 | bytes 8388608 | tf_op jit(solution)/shard_map/concatenate | solution.py:48
  140.4 10.0 %gather_fusion.1 = f32[48,256,256]{2,1,0:T(8,128)} fusion(f32[16,256,256]{2,1,0:T(8,128)} %pad_maximum_fusion, s32[1024]{0:T(1024)S(1)} %pad_clamp_fusion), kind=kCustom, calls=%fused_computation.1 | custom fusion | bytes 25166016 | tf_op jit(solution)/shard_map/gather | solution.py:52
  150.3 3.9 %all-gather.8.cloned.1.call-done = f32[1024,256]{0,1:T(8,128)} async-done(((f32[128,256]{0,1:T(8,128)}), f32[1024,256]{0,1:T(8,128)}) %all-gather.8.cloned.1.call-update) | async-done | bytes 1048592 | tf_op jit(solution)/shard_map/all_gather | solution.py:37
  154.2 1.6 copy.34
  155.8 0.6 gather_fusion
  156.4 0.6 convolution_bitcast_fusion
  157.0 21.9 %all-gather.10.cloned.1.call-done = f32[1024,256]{0,1:T(8,128)} async-done(((f32[128,256]{0,1:T(8,128)}), f32[1024,256]{0,1:T(8,128)}) %all-gather.10.cloned.1.call-update) | async-done | bytes 1048592 | tf_op jit(solution)/shard_map/all_gather | solution.py:44
  178.9 1.4 copy.35
  180.3 0.3 bitcast_reduce_fusion
  180.6 0.3 fusion.3
  180.9 1.4 fusion.16
  182.3 2.9 %fusion.1 = f32[12,256,256]{2,1,0:T(8,128)S(1)} fusion(f32[12,256,128]{2,1,0:T(8,128)S(1)} %copy-done, f32[256,12,128]{2,0,1:T(8,128)S(1)} %fusion.16), kind=kOutput, calls=%fused_computation.5 | convolution fusion | flops 1207959552 | bytes 6291456 | tf_op jit(solution)/shard_map/lpk,lkv->lpv/dot_general | solution.py:47
  185.2 27.0 %fusion = f32[12,256,256]{1,2,0:T(8,128)} fusion(f32[12,256,256]{2,1,0:T(8,128)S(1)} %fusion.1, f32[12,4,256,256]{3,2,1,0:T(8,128)} %bitcast.67, f32[12,4,256,256]{3,2,1,0:T(8,128)} %param.22), kind=kOutput, calls=%fused_computation.4 | convolution fusion | flops 9664462848 | bytes 31457280 | tf_op jit(solution)/shard_map/ljpq,ljpv->lqv/dot_general | solution.py:53
  212.2 3.5 %copy.28 = f32[12,256,256]{2,1,0:T(8,128)} copy(f32[12,256,256]{1,2,0:T(8,128)} %fusion) | data formatting | bytes 6291456 | tf_op jit(solution)/shard_map/add | solution.py:54
  (28 shorter events, 0.1 us)
Async XLA Ops:
  6.5 175.7 %copy-start = (f32[12,256,128]{2,1,0:T(8,128)S(1)}, f32[12,256,128]{2,1,0:T(8,128)}, u32[]{:S(2)}) copy-start(f32[12,256,128]{2,1,0:T(8,128)} %param.15) | copy-start | bytes 4718596
  6.5 7.7 %copy-start.2 = (f32[12,128,128]{2,1,0:T(8,128)S(1)}, f32[12,128,128]{2,1,0:T(8,128)}, u32[]{:S(2)}) copy-start(f32[12,128,128]{2,1,0:T(8,128)} %param.16) | copy-start | bytes 2359300
  6.5 9.2 %copy-start.5 = (f32[1,128,128]{2,1,0:T(8,128)S(1)}, f32[1,128,128]{2,1,0:T(8,128)}, u32[]{:S(2)}) copy-start(f32[1,128,128]{2,1,0:T(8,128)} %param.17) | copy-start | bytes 196612
  6.5 72.1 %all-reduce.2.cloned.1.call-start = ((), (), s32[]{:S(2)}) async-start(), calls=%async_computation | async-start | bytes 262144 | tf_op jit(solution)/shard_map/psum | solution.py:38
  14.3 111.0 %copy-start.6 = (f32[1,1,128,128]{3,2,1,0:T(8,128)S(1)}, f32[1,1,128,128]{3,2,1,0:T(8,128)}, u32[]{:S(2)}) copy-start(f32[1,1,128,128]{3,2,1,0:T(8,128)} %param.19) | copy-start | bytes 196612
  14.3 117.9 %copy-start.8 = (s32[12,4]{0,1:T(4,128)S(1)}, s32[12,4]{0,1:T(4,128)}, u32[]{:S(2)}) copy-start(s32[12,4]{0,1:T(4,128)} %param.23) | copy-start | bytes 580
  14.3 118.1 %copy-start.9 = (s32[1,2]{1,0:T(1,128)S(1)}, s32[1,2]{1,0:T(1,128)}, u32[]{:S(2)}) copy-start(s32[1,2]{1,0:T(1,128)} %param.24) | copy-start | bytes 28
  15.7 64.6 %copy-start.1 = (f32[256,128,1]{1,0,2:T(8,128)}, f32[256,128,1]{1,0,2:T(8,128)S(1)}, u32[]{:S(2)}) copy-start(f32[256,128,1]{1,0,2:T(8,128)S(1)} %fusion.15) | copy-start | bytes 393220
  16.7 108.6 %all-gather.6.cloned.1.call-start = ((), (), s32[]{:S(2)}) async-start(), calls=%async_computation.1 | async-start | bytes 2228224 | tf_op jit(solution)/shard_map/all_gather | solution.py:41
  80.3 73.9 %all-gather.8.cloned.1.call-start = ((), (), s32[]{:S(2)}) async-start(), calls=%async_computation.2 | async-start | bytes 1179648 | tf_op jit(solution)/shard_map/all_gather | solution.py:37
  81.0 97.8 %all-gather.10.cloned.1.call-start = ((), (), s32[]{:S(2)}) async-start(), calls=%async_computation.3 | async-start | bytes 1179648 | tf_op jit(solution)/shard_map/all_gather | solution.py:44
  129.3 3.1 %collective-permute-start = (f32[2,256,256]{2,1,0:T(8,128)}, f32[2,256,256]{2,1,0:T(8,128)S(1)}, u32[]{:S(2)}, u32[]{:S(2)}) collective-permute-start(f32[2,256,256]{2,1,0:T(8,128)} %get-tuple-element.16), channel_id=1, source_target_pairs={{0,1},{1,2},{2,3},{3,4},{4,5},{5,6},{6,7},{7,8},{8,9},{9,10},{10,1... | collective-permute-start | bytes 1572872 | tf_op jit(solution)/shard_map/ppermute | solution.py:13
  130.7 5.5 %collective-permute-start.1 = (f32[2,256,256]{2,1,0:T(8,128)S(1)}, f32[2,256,256]{2,1,0:T(8,128)S(1)}, u32[]{:S(2)}, u32[]{:S(2)}) collective-permute-start(f32[2,256,256]{2,1,0:T(8,128)S(1)} %get-tuple-element.17), channel_id=1, source_target_pairs={{1,0},{2,1},{3,2},{4,3},{5,4},{6,5},{7,6},{8,7},{9,8},{10,9},{11,1... | collective-permute-start | bytes 1572872 | tf_op jit(solution)/shard_map/ppermute | solution.py:13
  140.4 16.0 %copy-start.4 = (f32[1,2,128,128]{3,2,1,0:T(8,128)S(1)}, f32[1,2,128,128]{3,2,1,0:T(8,128)}, u32[]{:S(2)}) copy-start(f32[1,2,128,128]{3,2,1,0:T(8,128)} %param.18) | copy-start | bytes 393220
  150.3 30.2 %copy-start.7 = (f32[1,128,128]{2,1,0:T(8,128)S(1)}, f32[1,128,128]{2,1,0:T(8,128)}, u32[]{:S(2)}) copy-start(f32[1,128,128]{2,1,0:T(8,128)} %param.20) | copy-start | bytes 196612
  156.4 24.5 %copy-start.3 = (f32[12,128,128]{2,1,0:T(8,128)S(1)}, f32[12,128,128]{2,1,0:T(8,128)}, u32[]{:S(2)}) copy-start(f32[12,128,128]{2,1,0:T(8,128)} %param.21) | copy-start | bytes 2359300
Sparse Core Ops, SparseCore 0:
  16.8 61.7 all-reduce.1
  81.0 44.2 all-gather.5
  127.1 27.0 all-gather.7
  155.9 22.9 all-gather.9
